TPU v7x, 32 devices: a whole 2x2x4 slice. The times are simulated.
32 devices in a mesh: blk: 16 (over z, y, core), group: 2 (over x).
Axes of the slice: x: 2, y: 2, z: 4, core: 2. Of those that a mesh axis runs over, the one named last changes fastest.
Arguments:
- image_feats: bfloat16 [4096, 768], P(('blk', 'group')), may hold values from -0.796875 to 0.796875
- text_feats: bfloat16 [4096, 768], P(('blk', 'group')), may hold values from -0.796875 to 0.796875
- image_proj: bfloat16 [768, 768], replicated, may hold values from -0.21875 to 0.21875
- text_proj: bfloat16 [768, 768], replicated, may hold values from -0.21875 to 0.21875
- logit_scale: float32 [1], replicated, may hold values from 5 to 20
- logit_bias: float32 [1], replicated, may hold values from -3 to 0
- match: int32 [4096], P(('blk', 'group')), may hold values from 0 to 4095, as said below
Outputs:
- grad_image_feats: bfloat16 [4096, 768], P(('blk', 'group'))
- grad_text_feats: bfloat16 [4096, 768], P(('blk', 'group'))
Inputs may be any that keep to these rules, and one draw needn't show every extreme that they name: match of an image row in block b (rows b * 2 * 128 to (b + 1) * 2 * 128 - 1) names a report row of one of the blocks (b - k) mod 16, k below 4.
All inputs are finite; a program needn't handle non-finite values.
Results may differ from a plain program's by a relative error of at most 0.02.
Values may be sent and summed in bfloat16 or wider, within the bound.
A program may use at most 64 MiB of HBM per device.

v0:
```python
import functools

import jax
import jax.numpy as jnp
from jax import lax
from jax.experimental import pallas as pl
from jax.experimental.pallas import tpu as pltpu
from jax.sharding import PartitionSpec as P

MESH = pl.DeviceIdType.MESH
SPAN = 4
OWN, AT_A, AT_C, AT_B = range(SPAN)
CHUNKS = 2
A, B, C, R, A2, B2, C2, R2 = range(0, 8 * CHUNKS, CHUNKS)
X, M, X2 = range(8 * CHUNKS, 8 * CHUNKS + 3)
SEMS = 8 * CHUNKS + 3


def embed(feats, proj):
    x = jnp.dot(feats, proj, preferred_element_type=jnp.float32)
    inv = lax.rsqrt(jnp.sum(x * x, axis=-1, keepdims=True) + 1e-06)
    return x * inv, inv


def back_norm(grad, unit, inv, turned):
    inner = jnp.sum(grad * unit, axis=-1, keepdims=True)
    grad_x = (inv * (grad - inner * unit)).astype(jnp.bfloat16)
    out = jnp.dot(grad_x, turned, preferred_element_type=jnp.float32)
    return out.astype(jnp.bfloat16)


def kernel(
    n,
    image_feats, text_feats, image_proj, text_proj, scale_ref, bias_ref, match,
    out,
    feats_i, feats_t, proj_i, proj_t, turned_i, turned_t,
    unit_i, inv_i, unit_t, inv_t, images, images_turned, texts, coefs, match_nbr,
    gt_own, gt_a, gt_b, send_a, send_b, send_c, send_x,
    got_a, got_b, got_c, got_r, got_x,
    load_sem, send_sem, recv_sem,
):
    rows = match.shape[1]
    step = rows // CHUNKS
    blk = lax.axis_index("blk")
    grp = lax.axis_index("group")
    odd = lax.rem(blk, 2)
    q = lax.rem(blk, 4)

    def at(distance):
        return lax.rem(blk + distance + n, n)

    sibling = blk + 1 - 2 * odd
    across = (blk, 1 - grp)
    from_a, from_b, from_c = at(-2), at(2 * odd - 3), at(-1 - 2 * odd)

    loads = [
        pltpu.make_async_copy(src, dst, load_sem.at[i])
        for i, (src, dst) in enumerate(
            (
                (text_feats, feats_t),
                (text_proj, proj_t),
                (image_feats, feats_i),
                (image_proj, proj_i),
            )
        )
    ]
    for load in loads:
        load.start()

    barrier = pltpu.get_barrier_semaphore()

    def greet(partner):
        pl.semaphore_signal(barrier, inc=1, device_id=partner, device_id_type=MESH)

    greet((sibling, grp))
    greet(across)
    greet((at(6 * odd - 3), grp))
    pl.when(q != 3)(lambda: greet((at(2), grp)))
    pl.when(q != 1)(lambda: greet((at(-2), grp)))
    pl.when(q == 1)(lambda: greet((at(1), grp)))
    pl.when(q == 2)(lambda: greet((at(-1), grp)))

    def remote(send, recv, src, dst, partner):
        return pltpu.make_async_remote_copy(
            src_ref=src, dst_ref=dst, send_sem=send_sem.at[send],
            recv_sem=recv_sem.at[recv], device_id=partner, device_id_type=MESH,
        )

    def part(i):
        return pl.ds(i * step, step)

    def between(send, recv, src, dst, partner):
        return [
            remote(send + i, recv + i, src.at[part(i)], dst.at[part(i)], partner)
            for i in range(CHUNKS)
        ]

    def start(copies):
        for copy in copies:
            copy.start()

    def wait_recv(copies):
        for copy in copies:
            copy.wait_recv()

    def wait_send(copies):
        for copy in copies:
            copy.wait_send()

    def slot(place):
        return texts.at[pl.ds(place * rows, rows)]

    loads[0].wait()
    loads[1].wait()
    unit, inv = embed(feats_t[...], proj_t[...])
    texts[:rows, :] = unit.astype(jnp.bfloat16)

    pl.semaphore_wait(barrier, 5 + (q == 2).astype(jnp.int32) - (q == 3).astype(jnp.int32))
    copy_a = between(A, A, slot(OWN), slot(AT_A), (at(2), grp))
    copy_b = between(B, B, slot(OWN), slot(AT_B), (at(1 + 2 * odd), grp))
    copy_c = between(C, C, slot(AT_A), slot(AT_C), (sibling, grp))
    relay = between(R, A, slot(AT_B), slot(AT_A), (at(-1), grp))
    copy_m = remote(M, M, match, match_nbr, across)
    pl.when(q != 3)(lambda: start(copy_a))
    start(copy_b)
    copy_m.start()
    unit_t[...] = unit
    inv_t[...] = inv

    loads[2].wait()
    loads[3].wait()
    unit, inv = embed(feats_i[...], proj_i[...])
    images[:rows, :] = unit.astype(jnp.bfloat16)
    copy_x = remote(X, X, images.at[pl.ds(0, rows)], images.at[pl.ds(rows, rows)], across)
    copy_x.start()
    unit_i[...] = unit
    inv_i[...] = inv
    turned_t[...] = proj_t[...].T
    turned_i[...] = proj_i[...].T

    scale = scale_ref[0]
    bias = bias_ref[0]

    def pair(place, source):
        ids = (source * 2 + grp) * rows + lax.broadcasted_iota(
            jnp.int32, (rows, 2 * rows), 0
        )
        wanted = jnp.concatenate([match[...], match_nbr[...]], axis=1)
        hit = wanted == ids
        here = slice(place * rows, (place + 1) * rows)
        logits = (
            scale
            * jnp.dot(texts[here, :], images_turned[...], preferred_element_type=jnp.float32)
            + bias
        )
        weight = jax.nn.sigmoid(jnp.where(hit, -logits, logits)) * scale
        coef = jnp.where(hit, -weight, weight).astype(jnp.bfloat16)
        coefs[here, :] = coef
        return jnp.dot(coef, images[...], preferred_element_type=jnp.float32)

    def image_grad(which):
        return lax.dot_general(
            coefs[:, which], texts[...], (((0,), (0,)), ((), ())),
            preferred_element_type=jnp.float32,
        )

    back_a = between(A2, A2, send_a, got_a, (from_a, grp))
    back_r = between(A2, R2, send_a, got_r, (at(1), grp))
    back_b = between(B2, B2, send_b, got_b, (from_b, grp))
    back_c = between(C2, C2, send_c, got_c, (sibling, grp))
    back_x = remote(X2, X2, send_x, got_x, across)

    def pass_on(come, go):
        for i in range(CHUNKS):
            come[i].wait_recv()
            go[i].start()

    def finish_b():
        wait_recv(copy_b)
        send_b[...] = pair(AT_B, from_b).astype(jnp.bfloat16)
        start(back_b)

    def relayed_b():
        gt_b[...] = pair(AT_B, from_b)

    def relay_back():
        for i in range(CHUNKS):
            back_r[i].wait_recv()
            send_b[part(i), :] = (
                gt_b[part(i), :] + got_r[part(i), :].astype(jnp.float32)
            ).astype(jnp.bfloat16)
            back_b[i].start()

    pl.when(q == 2)(lambda: pass_on(copy_b, relay))
    pl.when(q != 1)(lambda: pass_on(copy_a, copy_c))

    copy_m.wait()
    copy_x.wait()
    images_turned[...] = images[...].T
    gt_own[...] = pair(OWN, blk)

    pl.when(odd == 1)(finish_b)
    pl.when(q == 1)(lambda: pass_on(copy_a, copy_c))

    gt_a[...] = pair(AT_A, from_a)
    wait_recv(copy_c)
    send_c[...] = pair(AT_C, from_c).astype(jnp.bfloat16)
    start(back_c)

    for i in range(CHUNKS):
        back_c[i].wait_recv()
        send_a[part(i), :] = (
            gt_a[part(i), :] + got_c[part(i), :].astype(jnp.float32)
        ).astype(jnp.bfloat16)
        pl.when(q == 1)(back_r[i].start)
        pl.when(q != 1)(back_a[i].start)

    pl.when(q == 0)(finish_b)
    pl.when(q == 2)(relayed_b)

    send_x[...] = image_grad(slice(rows, 2 * rows)).astype(jnp.bfloat16)
    back_x.start()
    pl.when(q == 2)(relay_back)
    grad = image_grad(slice(0, rows))

    back_x.wait_recv()
    grad = grad + got_x[...].astype(jnp.float32)
    out[:rows, :] = back_norm(grad, unit_i[...], inv_i[...], turned_i[...])

    def add_a():
        wait_recv(back_a)
        gt_own[...] += got_a[...].astype(jnp.float32)

    wait_recv(back_b)
    gt_own[...] += got_b[...].astype(jnp.float32)
    pl.when(q != 3)(add_a)
    out[rows:, :] = back_norm(gt_own[...], unit_t[...], inv_t[...], turned_t[...])

    pl.when(q != 3)(lambda: wait_send(copy_a))
    pl.when(q == 2)(lambda: wait_send(relay))
    for copies in (copy_b, copy_c, back_a, back_b, back_c, [back_x]):
        wait_send(copies)


def body(image_feats, text_feats, image_proj, text_proj, logit_scale, logit_bias, match):
    n = lax.axis_size("blk")
    rows, depth = image_feats.shape
    half = lambda *shape: pltpu.VMEM(shape, jnp.bfloat16)
    full = lambda *shape: pltpu.VMEM(shape, jnp.float32)
    far = pl.BlockSpec(memory_space=pltpu.HBM)
    near = pl.BlockSpec(memory_space=pltpu.VMEM)
    scalar = pl.BlockSpec(memory_space=pltpu.SMEM)
    tile = (rows, depth)
    both = pl.pallas_call(
        functools.partial(kernel, n),
        out_shape=jax.ShapeDtypeStruct((2 * rows, depth), jnp.bfloat16),
        in_specs=[far] * 4 + [scalar] * 2 + [near],
        out_specs=near,
        scratch_shapes=[
            half(*tile), half(*tile), half(depth, depth), half(depth, depth),
            half(depth, depth), half(depth, depth),
            full(*tile), full(rows, 1), full(*tile), full(rows, 1),
            half(2 * rows, depth), half(depth, 2 * rows),
            half(SPAN * rows, depth), half(SPAN * rows, 2 * rows),
            pltpu.VMEM((1, rows), jnp.int32),
            full(*tile), full(*tile), full(*tile),
            half(*tile), half(*tile), half(*tile), half(*tile),
            half(*tile), half(*tile), half(*tile), half(*tile), half(*tile),
            pltpu.SemaphoreType.DMA((4,)),
            pltpu.SemaphoreType.DMA((SEMS,)),
            pltpu.SemaphoreType.DMA((SEMS,)),
        ],
        compiler_params=pltpu.CompilerParams(
            collective_id=0, has_side_effects=True, vmem_limit_bytes=64 * 1024 * 1024
        ),
        cost_estimate=pl.CostEstimate(
            flops=8 * rows * depth * depth + 48 * rows * rows * depth,
            bytes_accessed=4 * depth * depth + 8 * rows * depth,
            transcendentals=8 * rows * rows,
        ),
    )(
        image_feats, text_feats, image_proj, text_proj, logit_scale, logit_bias,
        match.reshape(1, rows),
    )
    return both[:rows], both[rows:]


def solution(mesh):
    rows = P(("blk", "group"), None)
    return jax.shard_map(
        body,
        mesh=mesh,
        in_specs=(rows, rows, P(), P(), P(), P(), P(("blk", "group"))),
        out_specs=(rows, rows),
        check_vma=False,
    )
```

profile of v0, /device:TPU:0, one launch (start us, length us, event | category | flops | bytes accessed | tf_op | source)
XLA Modules:
  0.0 31.4 jit_solution(4789563454371350599)
XLA Ops:
  1.9 27.6 %shard_map.86 = bf16[256,768]{1,0:T(8,128)(2,1)} custom-call(bf16[128,768]{1,0:T(8,128)(2,1)} %image_feats.1, bf16[128,768]{1,0:T(8,128)(2,1)} %text_feats.1, bf16[768,768]{1,0:T(8,128)(2,1)} %image_proj.1, bf16[768,768]{1,0:T(8,128)(2,1)} %text_proj.1, f32[1]{0:T(128)S(6)} %copy.9.scale_ref, f32[1]{0:T(128)S(6)} %copy.10.bias_ref, s32[1,128]{1,0:T(1,128)} %bitcast.1), custom_call_target="tpu_custom_call" | custom-call | flops 1207959552 | bytes 3145728 | tf_op jit(solution)/shard_map/pallas_call | solution.py:254
  29.6 1.8 %fusion = (bf16[128,768]{1,0:T(8,128)(2,1)}, bf16[128,768]{1,0:T(8,128)(2,1)}) fusion(bf16[256,768]{1,0:T(8,128)(2,1)} %shard_map.86), kind=kLoop, calls=%fused_computation | loop fusion | bytes 786432 | tf_op jit(solution)/shard_map/slice | solution.py:285
where the time goes:
time: 31.6 us; the launch traced here: 31.4 us
  Pallas kernels  27.6 us (87%)
  between operations  1.93 us (6%)
  local copies, waits for them, and re-layouts  1.79 us (6%)
    pallas_call x1, Pallas kernels, body(): pl.pallas_call(functools.partial(kernel, n), out_shape=jax.ShapeDtypeStru...  27.6 us
    slice x1, local copies, waits for them, and re-layouts, body(): return (both[:rows], both[rows:])  1.79 us

commit v1 on v0

v1 whole, which is shorter than its diff:
```python
import functools

import jax
import jax.numpy as jnp
from jax import lax
from jax.experimental import pallas as pl
from jax.experimental.pallas import tpu as pltpu
from jax.sharding import PartitionSpec as P

MESH = pl.DeviceIdType.MESH
SPAN = 4
OWN, AT_A, AT_C, AT_B = range(SPAN)
CHUNKS = 2
A, C, A2, C2 = range(0, 4 * CHUNKS, CHUNKS)
B, B2, X, M, X2 = range(4 * CHUNKS, 4 * CHUNKS + 5)
SEMS = 4 * CHUNKS + 5


def embed(feats, proj):
    x = jnp.dot(feats, proj, preferred_element_type=jnp.float32)
    inv = lax.rsqrt(jnp.sum(x * x, axis=-1, keepdims=True) + 1e-06)
    return x * inv, inv


def back_norm(grad, unit, inv, turned):
    inner = jnp.sum(grad * unit, axis=-1, keepdims=True)
    grad_x = (inv * (grad - inner * unit)).astype(jnp.bfloat16)
    out = jnp.dot(grad_x, turned, preferred_element_type=jnp.float32)
    return out.astype(jnp.bfloat16)


def kernel(
    n,
    image_feats, text_feats, image_proj, text_proj, matches, scale_ref, bias_ref,
    out,
    feats_i, feats_t, proj_i, proj_t, turned_i, turned_t,
    unit_i, inv_i, unit_t, inv_t, images, images_turned, texts, coefs, match, match_nbr,
    gt_own, gt_a, send_a, send_b, send_c, send_x,
    got_a, got_b, got_c, got_x,
    load_sem, send_sem, recv_sem,
):
    rows = match.shape[1]
    step = rows // CHUNKS
    blk = lax.axis_index("blk")
    grp = lax.axis_index("group")
    odd = lax.rem(blk, 2)

    def at(distance):
        return lax.rem(blk + distance + n, n)

    sibling = blk + 1 - 2 * odd
    across = (blk, 1 - grp)
    from_a, from_b, from_c = at(-2), at(2 * odd - 3), at(-1 - 2 * odd)

    loads = [
        pltpu.make_async_copy(src, dst, load_sem.at[i])
        for i, (src, dst) in enumerate(
            (
                (text_feats, feats_t),
                (text_proj, proj_t),
                (image_feats, feats_i),
                (image_proj, proj_i),
                (matches, match),
            )
        )
    ]
    loads[0].start()
    loads[1].start()
    loads[4].start()

    barrier = pltpu.get_barrier_semaphore()

    def greet(partner):
        pl.semaphore_signal(barrier, inc=1, device_id=partner, device_id_type=MESH)

    greet((sibling, grp))
    greet(across)
    greet((at(6 * odd - 3), grp))
    greet((at(2), grp))
    greet((at(-2), grp))

    def remote(role, src, dst, partner):
        return pltpu.make_async_remote_copy(
            src_ref=src, dst_ref=dst, send_sem=send_sem.at[role],
            recv_sem=recv_sem.at[role], device_id=partner, device_id_type=MESH,
        )

    def part(i):
        return pl.ds(i * step, step)

    def between(role, src, dst, partner):
        return [
            remote(role + i, src.at[part(i)], dst.at[part(i)], partner)
            for i in range(CHUNKS)
        ]

    def start(copies):
        for copy in copies:
            copy.start()

    def wait_recv(copies):
        for copy in copies:
            copy.wait_recv()

    def wait_send(copies):
        for copy in copies:
            copy.wait_send()

    def slot(place):
        return texts.at[pl.ds(place * rows, rows)]

    loads[0].wait()
    loads[1].wait()
    loads[2].start()
    loads[3].start()
    unit, inv = embed(feats_t[...], proj_t[...])
    texts[:rows, :] = unit.astype(jnp.bfloat16)

    pl.semaphore_wait(barrier, 5)
    copy_a = between(A, slot(OWN), slot(AT_A), (at(2), grp))
    copy_b = remote(B, slot(OWN), slot(AT_B), (at(1 + 2 * odd), grp))
    copy_c = between(C, slot(AT_A), slot(AT_C), (sibling, grp))
    copy_m = remote(M, match, match_nbr, across)
    start(copy_a)
    copy_b.start()
    loads[4].wait()
    copy_m.start()
    unit_t[...] = unit
    inv_t[...] = inv

    loads[2].wait()
    loads[3].wait()
    unit, inv = embed(feats_i[...], proj_i[...])
    images[:rows, :] = unit.astype(jnp.bfloat16)
    copy_x = remote(X, images.at[pl.ds(0, rows)], images.at[pl.ds(rows, rows)], across)
    copy_x.start()
    unit_i[...] = unit
    inv_i[...] = inv
    turned_t[...] = proj_t[...].T
    turned_i[...] = proj_i[...].T

    scale = scale_ref[0]
    bias = bias_ref[0]

    def pair(place, source):
        ids = (source * 2 + grp) * rows + lax.broadcasted_iota(
            jnp.int32, (rows, 2 * rows), 0
        )
        wanted = jnp.concatenate([match[...], match_nbr[...]], axis=1)
        hit = wanted == ids
        here = slice(place * rows, (place + 1) * rows)
        logits = (
            scale
            * jnp.dot(texts[here, :], images_turned[...], preferred_element_type=jnp.float32)
            + bias
        )
        weight = jax.nn.sigmoid(jnp.where(hit, -logits, logits)) * scale
        coef = jnp.where(hit, -weight, weight).astype(jnp.bfloat16)
        coefs[here, :] = coef
        return jnp.dot(coef, images[...], preferred_element_type=jnp.float32)

    def image_grad(which):
        return lax.dot_general(
            coefs[:, which], texts[...], (((0,), (0,)), ((), ())),
            preferred_element_type=jnp.float32,
        )

    back_a = between(A2, send_a, got_a, (from_a, grp))
    back_b = remote(B2, send_b, got_b, (from_b, grp))
    back_c = between(C2, send_c, got_c, (sibling, grp))
    back_x = remote(X2, send_x, got_x, across)

    def pass_on(come, go):
        for i in range(CHUNKS):
            come[i].wait_recv()
            go[i].start()

    def finish_b():
        copy_b.wait_recv()
        send_b[...] = pair(AT_B, from_b).astype(jnp.bfloat16)
        back_b.start()

    pass_on(copy_a, copy_c)
    copy_m.wait()
    copy_x.wait()
    images_turned[...] = images[...].T
    gt_own[...] = pair(OWN, blk)

    pl.when(odd == 1)(finish_b)

    gt_a[...] = pair(AT_A, from_a)
    wait_recv(copy_c)
    send_c[...] = pair(AT_C, from_c).astype(jnp.bfloat16)
    start(back_c)

    for i in range(CHUNKS):
        back_c[i].wait_recv()
        send_a[part(i), :] = (
            gt_a[part(i), :] + got_c[part(i), :].astype(jnp.float32)
        ).astype(jnp.bfloat16)
        back_a[i].start()

    pl.when(odd == 0)(finish_b)

    send_x[...] = image_grad(slice(rows, 2 * rows)).astype(jnp.bfloat16)
    back_x.start()
    grad = image_grad(slice(0, rows))

    back_x.wait_recv()
    grad = grad + got_x[...].astype(jnp.float32)
    out[:rows, :] = back_norm(grad, unit_i[...], inv_i[...], turned_i[...])

    back_b.wait_recv()
    gt_own[...] += got_b[...].astype(jnp.float32)
    wait_recv(back_a)
    grad = gt_own[...] + got_a[...].astype(jnp.float32)
    out[rows:, :] = back_norm(grad, unit_t[...], inv_t[...], turned_t[...])

    for copies in (copy_a, [copy_b], copy_c, back_a, [back_b], back_c, [back_x]):
        wait_send(copies)


def body(image_feats, text_feats, image_proj, text_proj, logit_scale, logit_bias, match):
    n = lax.axis_size("blk")
    rows, depth = image_feats.shape
    half = lambda *shape: pltpu.VMEM(shape, jnp.bfloat16)
    full = lambda *shape: pltpu.VMEM(shape, jnp.float32)
    far = pl.BlockSpec(memory_space=pltpu.HBM)
    near = pl.BlockSpec(memory_space=pltpu.VMEM)
    scalar = pl.BlockSpec(memory_space=pltpu.SMEM)
    tile = (rows, depth)
    both = pl.pallas_call(
        functools.partial(kernel, n),
        out_shape=jax.ShapeDtypeStruct((2 * rows, depth), jnp.bfloat16),
        in_specs=[far] * 5 + [scalar] * 2,
        out_specs=near,
        scratch_shapes=[
            half(*tile), half(*tile), half(depth, depth), half(depth, depth),
            half(depth, depth), half(depth, depth),
            full(*tile), full(rows, 1), full(*tile), full(rows, 1),
            half(2 * rows, depth), half(depth, 2 * rows),
            half(SPAN * rows, depth), half(SPAN * rows, 2 * rows),
            pltpu.VMEM((1, rows), jnp.int32), pltpu.VMEM((1, rows), jnp.int32),
            full(*tile), full(*tile),
            half(*tile), half(*tile), half(*tile), half(*tile),
            half(*tile), half(*tile), half(*tile), half(*tile),
            pltpu.SemaphoreType.DMA((5,)),
            pltpu.SemaphoreType.DMA((SEMS,)),
            pltpu.SemaphoreType.DMA((SEMS,)),
        ],
        compiler_params=pltpu.CompilerParams(
            collective_id=0, has_side_effects=True, vmem_limit_bytes=32 * 1024 * 1024
        ),
        cost_estimate=pl.CostEstimate(
            flops=8 * rows * depth * depth + 48 * rows * rows * depth,
            bytes_accessed=4 * depth * depth + 8 * rows * depth,
            transcendentals=8 * rows * rows,
        ),
    )(
        *(
            pltpu.with_memory_space_constraint(x, pltpu.HBM)
            for x in (image_feats, text_feats, image_proj, text_proj, match.reshape(1, rows))
        ),
        logit_scale, logit_bias,
    )
    return both[:rows], both[rows:]


def solution(mesh):
    rows = P(("blk", "group"), None)
    return jax.shard_map(
        body,
        mesh=mesh,
        in_specs=(rows, rows, P(), P(), P(), P(), P(("blk", "group"))),
        out_specs=(rows, rows),
        check_vma=False,
    )
```

time: 31.6 us -> 27.8 us (0.88)
  Pallas kernels: 27.6 us -> 25 us
  local copies, waits for them, and re-layouts: 1.79 us -> 0.77 us
    pallas_call x1, Pallas kernels: 27.6 us -> 25 us  [body(): pl.pallas_call(functools.partial(kernel, n), out_shape=jax.ShapeDtypeStru...]
    slice x1, local copies, waits for them, and re-layouts: 1.79 us -> 0.77 us  [body(): return (both[:rows], both[rows:])]
where the time goes in v1:
time: 27.8 us; the launch traced here: 27.7 us
  Pallas kernels  25 us (90%)
  between operations  1.93 us (7%)
  local copies, waits for them, and re-layouts  0.77 us (3%)
    pallas_call x1, Pallas kernels, body(): pl.pallas_call(functools.partial(kernel, n), out_shape=jax.ShapeDtypeStru...  25 us
    slice x1, local copies, waits for them, and re-layouts, body(): return (both[:rows], both[rows:])  0.77 us

profile of v1, /device:TPU:0, one launch (start us, length us, event | category | flops | bytes accessed | tf_op | source)
XLA Modules:
  0.0 27.7 jit_solution(11656897151763370525)
XLA Ops:
  1.9 25.0 %shard_map.86 = bf16[256,768]{1,0:T(8,128)(2,1)S(1)} custom-call(bf16[128,768]{1,0:T(8,128)(2,1)} %image_feats.1, bf16[128,768]{1,0:T(8,128)(2,1)} %text_feats.1, bf16[768,768]{1,0:T(8,128)(2,1)} %image_proj.1, bf16[768,768]{1,0:T(8,128)(2,1)} %text_proj.1, s32[1,128]{1,0:T(1,128)} %bitcast.1, f32[1]{0:T(128)S(6)} %copy.9.scale_ref, f32[1]{0:T(128)S(6)} %copy.10.bias_ref), custom_call_target="tpu_custom_call" | custom-call | flops 1207959552 | bytes 3145728 | tf_op jit(solution)/shard_map/pallas_call | solution.py:232
  26.9 0.8 %fusion = (bf16[128,768]{1,0:T(8,128)(2,1)}, bf16[128,768]{1,0:T(8,128)(2,1)}) fusion(bf16[256,768]{1,0:T(8,128)(2,1)S(1)} %shard_map.86), kind=kLoop, calls=%fused_computation | loop fusion | bytes 786432 | tf_op jit(solution)/shard_map/slice | solution.py:266
